TPU v7x, 128 devices: a whole 4x4x4 slice. The times are simulated.
128 devices in a mesh: energy: 32 (over z, y, core), section: 4 (over x).
Axes of the slice: x: 4, y: 4, z: 4, core: 2. Of those that a mesh axis runs over, the one named last changes fastest.
Arguments:
- onsite: float32 [8, 256], P('section'), may hold values from -1 to 1
- hopping: float32 [8, 256, 256], P('section'), may hold values from -0.125 to 0.125
- coupling: float32 [8, 256, 256], P('section'), may hold values from -4 to 4
- broadening: float32 [32], P('energy'), may hold values from 1.5 to 3
- born_sigma: float32 [32, 8, 2, 256, 256], P('energy', 'section'), may hold values from -0.046875 to 0.046875
- phonon_shift: int32 [4], replicated, may hold values from -2 to 2
- phonon_local: float32 [4, 256, 256], replicated, may hold values from 0.5 to 4
- phonon_side: float32 [4, 256, 256], replicated, may hold values from 0.2 to 2
Outputs:
- next_sigma: float32 [32, 8, 2, 256, 256], P('energy', 'section')
All inputs are finite; a program needn't handle non-finite values.
Results may differ from a plain program's by a relative error of at most 0.0001.
Values sent between devices are 32-bit elements; how exact they have to be, the bound alone decides.
A program may use at most 128 MiB of HBM per device.

v0:
```python
import jax
import jax.numpy as jnp
from jax import lax
from jax.experimental import pallas as pl
from jax.experimental.pallas import tpu as pltpu
from jax.sharding import PartitionSpec as P

MODES = 4
N = 256
F32 = jnp.float32
BF16 = jnp.bfloat16
MESH = pl.DeviceIdType.MESH

ORDERS = ((2, 3, 7, 5, 6, 0), (2, 3, 5, 4, 7, 6), (5, 4, 2, 3, 6, 7), (5, 4, 6, 2, 7, 0))
SLOTS = 6


def order_code(digits):
    return sum(d * 8**i for i, d in enumerate(digits))


def cat(parts, axis):
    return jnp.concatenate(parts, axis=axis)


def split(x):
    hi = x.astype(BF16)
    return hi, (x - hi.astype(F32)).astype(BF16)


def dot3(a, b):
    return jnp.dot(
        cat([a[0], a[1], a[0]], 1), cat([b[0], b[0], b[1]], 0), preferred_element_type=F32
    )


def halves(re, im):
    return split(re), split(im), split(re + im)


def cdot(a, b):
    p1 = dot3(a[0], b[0])
    p2 = dot3(a[1], b[1])
    p3 = dot3(a[2], b[2])
    return p1 - p2, p3 - p1 - p2


def diagonal_mask():
    return lax.broadcasted_iota(jnp.int32, (N, N), 0) == lax.broadcasted_iota(jnp.int32, (N, N), 1)


def inverse(mr, mi):
    eye = diagonal_mask()

    def reciprocal(axis):
        dr = jnp.sum(jnp.where(eye, mr, 0.0), axis=axis, keepdims=True)
        di = jnp.sum(jnp.where(eye, mi, 0.0), axis=axis, keepdims=True)
        modulus = dr * dr + di * di
        return dr / modulus, -di / modulus

    xr, xi = reciprocal(0)
    rr = jnp.where(eye, 0.0, mi * xi - mr * xr)
    ri = jnp.where(eye, 0.0, -(mr * xi + mi * xr))
    r = halves(rr, ri)
    sr, si = cdot(r, r)
    s = halves(sr, si)
    tr, ti = cdot(s, s)
    yr = jnp.where(eye, 1.0, rr)
    ur, ui = cdot(halves(yr, ri), s)
    yr = yr + ur
    yi = ri + ui
    ur, ui = cdot(halves(yr, yi), halves(tr, ti))
    yr = yr + ur
    yi = yi + ui
    cr, ci = reciprocal(1)
    return yr * cr - yi * ci, yr * ci + yi * cr


def couple(a, gr, gi, b):
    gr, gi = split(gr), split(gi)
    g = (cat([gr[0], gi[0]], 1), cat([gr[1], gi[1]], 1))
    hi, lo = split(dot3(a, g))
    hi = cat([hi[:, :N], hi[:, N:]], 0)
    lo = cat([lo[:, :N], lo[:, N:]], 0)
    both = dot3((hi, lo), b)
    return both[:N], both[N:]


def kernel(
    onsite, hop, coup, broad, born, shift, ploc, pside, out,
    system, links, sig, green, hp, hm, ho, hf, wl, ws, ls, ss, sin,
    chain_s, chain_r, y_s, y_r, o_s, o_r, f_s, f_r, side_s, side_r, go,
):
    e = lax.axis_index("energy")
    s = lax.axis_index("section")
    core = lax.rem(e, 2)
    other = e + 1 - 2 * core
    has_p = e < 30
    has_m = e >= 2
    has_right = s < 3
    has_left = s > 0

    barrier = pltpu.get_barrier_semaphore()

    def greet(cond, where):
        @pl.when(cond)
        def _():
            pl.semaphore_signal(barrier, inc=1, device_id=where, device_id_type=MESH)

    greet(has_right, {"section": lax.rem(s + 1, 4)})
    greet(has_left, {"section": lax.rem(s + 3, 4)})
    greet(has_p, {"energy": lax.rem(e + 2, 32)})
    greet(has_m, {"energy": lax.rem(e + 30, 32)})
    pl.semaphore_signal(barrier, inc=1, device_id={"energy": other}, device_id_type=MESH)

    def remote(src, dst, ssem, rsem, where):
        return pltpu.make_async_remote_copy(
            src_ref=src, dst_ref=dst, send_sem=ssem, recv_sem=rsem, device_id=where, device_id_type=MESH
        )

    def left_copy():
        return remote(sig.at[5], sig.at[1], chain_s.at[0], chain_r.at[0], {"section": lax.rem(s + 1, 4)})

    def right_copy():
        return remote(green.at[2], sig.at[6], chain_s.at[1], chain_r.at[1], {"section": lax.rem(s + 3, 4)})

    def y_copy(up, b, part):
        if up:
            return remote(green.at[b, part], hm.at[b, part], y_s.at[0, b, part], y_r.at[0, b, part],
                          {"energy": lax.rem(e + 2, 32)})
        return remote(green.at[b, part], hp.at[b, part], y_s.at[1, b, part], y_r.at[1, b, part],
                      {"energy": lax.rem(e + 30, 32)})

    def own_copy(b, part):
        return remote(green.at[b, part], ho.at[b, part], o_s.at[b, part], o_r.at[b, part], {"energy": other})

    def fwd_copy(src, b, part):
        return remote(src.at[b, part], hf.at[b, part], f_s.at[b, part], f_r.at[b, part], {"energy": other})

    def side_right():
        return remote(ss.at[1], sin.at[0], side_s.at[1], side_r.at[0], {"section": lax.rem(s + 1, 4)})

    def side_left():
        return remote(ss.at[0], sin.at[1], side_s.at[0], side_r.at[1], {"section": lax.rem(s + 3, 4)})

    energy = -2.0 + 4.0 * e.astype(F32) / 31.0
    eta = broad[0]

    def setup(b, carry):
        eye = diagonal_mask()
        h = hop[b]
        ham = 0.5 * (h + h.T)
        system[b, 0] = jnp.where(eye, energy - onsite[pl.ds(b, 1), :], 0.0) - ham - born[0, b, 0]
        system[b, 1] = jnp.where(eye, eta, 0.0) - born[0, b, 1]
        v = coup[b]
        vh, vl = split(v)
        links[b, 0] = vh
        links[b, 1] = vl
        vh, vl = split(v.T)
        links[b, 2] = vh
        links[b, 3] = vl
        return carry

    lax.fori_loop(0, 2, setup, 0)
    sig[0] = jnp.zeros((2, N, N), F32)

    @pl.when(s == 0)
    def _():
        sig[1] = jnp.zeros((2, N, N), F32)

    @pl.when(s == 3)
    def _():
        sig[4] = jnp.zeros((2, N, N), F32)

    partners = (
        1 + has_right.astype(jnp.int32) + has_left.astype(jnp.int32)
        + has_p.astype(jnp.int32) + has_m.astype(jnp.int32)
    )
    pl.semaphore_wait(barrier, partners)

    def weights():
        def one(d, carry):
            wloc = jnp.zeros((N, N), F32)
            wside = jnp.zeros((N, N), F32)
            for k in range(MODES):
                on = jnp.where(shift[k] == d - 2, 1.0, 0.0)
                wloc = wloc + on * ploc[k]
                wside = wside + on * pside[k]
            wl[d] = wloc
            ws[d] = wside
            return carry

        lax.fori_loop(0, 5, one, 0)

    def at_section(values):
        return jnp.where(s == 0, values[0], jnp.where(s == 1, values[1], jnp.where(s == 2, values[2], values[3])))

    def slot(i, code):
        digit = lax.rem(code, 8)
        kind = digit // 2
        b = lax.rem(digit, 2)

        @pl.when(i == at_section((2, 0, 0, 2)))
        def _():
            weights()

        @pl.when(i == at_section((7, 0, 2, 2)))
        def _():
            left_copy().wait_recv()

        @pl.when(i == at_section((2, 2, 0, 7)))
        def _():
            right_copy().wait_recv()
            re, im = couple((links[1, 0], links[1, 1]), sig[6, 0], sig[6, 1], (links[1, 2], links[1, 3]))
            sig[4, 0] = re
            sig[4, 1] = im

        @pl.when(kind > 0)
        def _():
            first = jnp.where(kind == 2, 0, 1 + b)
            second = jnp.where(kind == 1, 0, 3 + b)
            place = jnp.where(kind == 3, b, jnp.where(digit == 4, 2, 3))
            re, im = inverse(
                system[b, 0] - sig[first, 0] - sig[second, 0], system[b, 1] - sig[first, 1] - sig[second, 1]
            )
            green[place, 0] = re
            green[place, 1] = im

            @pl.when((kind == 1) | (digit == 5))
            def _():
                v = jnp.where(kind == 1, b, 0)
                a0 = jnp.where(kind == 1, 2, 0)
                b0 = 2 - a0
                target = jnp.where(digit == 2, 2, jnp.where(digit == 3, 5, 3))
                re, im = couple((links[v, a0], links[v, a0 + 1]), green[3, 0], green[3, 1],
                                (links[v, b0], links[v, b0 + 1]))
                sig[target, 0] = re
                sig[target, 1] = im

            @pl.when((i == 1) & ((s == 0) | (s == 3)) & (core == 1))
            def _():
                pl.semaphore_wait(go, 1)

            @pl.when(digit == 3)
            def _():
                left_copy().start()

            @pl.when(digit == 4)
            def _():
                right_copy().start()

            @pl.when((i == 1) & (core == 0))
            def _():
                @pl.when(s == 0)
                def _():
                    left_copy().wait_send()

                @pl.when(s == 3)
                def _():
                    right_copy().wait_send()

                @pl.when((s == 0) | (s == 3))
                def _():
                    pl.semaphore_signal(go, inc=1, device_id={"energy": other}, device_id_type=MESH)

            @pl.when(kind == 3)
            def _():
                for part in range(2):
                    @pl.when(has_p)
                    def _():
                        y_copy(True, b, part).start()

                    @pl.when(has_m)
                    def _():
                        y_copy(False, b, part).start()

                    own_copy(b, part).start()

        return code // 8

    lax.fori_loop(0, SLOTS, slot, at_section([order_code(d) for d in ORDERS]))

    def units(t, carry):
        first = jnp.where(s < 2, 1, 0)
        half = t // 2
        b = first + half - 2 * first * half
        part = lax.rem(t, 2)

        def add(source, d):
            x = source[b, part]
            ls[b, part] = ls[b, part] + wl[d] * x
            ss[b, part] = ss[b, part] + ws[d] * x

        x = green[b, part]
        ls[b, part] = wl[2] * x
        ss[b, part] = ws[2] * x
        own_copy(b, part).wait_recv()
        add(ho, 3 - 2 * core)

        @pl.when(has_p)
        def _():
            y_copy(False, b, part).wait_recv()

            @pl.when(core == 0)
            def _():
                fwd_copy(hp, b, part).start()

            add(hp, 4)

        @pl.when(has_m)
        def _():
            y_copy(True, b, part).wait_recv()

            @pl.when(core == 1)
            def _():
                fwd_copy(hm, b, part).start()

            add(hm, 0)

        @pl.when(((core == 0) & has_m) | ((core == 1) & has_p))
        def _():
            fwd_copy(hp, b, part).wait_recv()
            add(hf, 1 + 2 * core)

        @pl.when(part == 1)
        def _():
            @pl.when((b == 1) & has_right)
            def _():
                side_right().start()

            @pl.when((b == 0) & has_left)
            def _():
                side_left().start()

        return carry

    lax.fori_loop(0, 4, units, 0)

    for b in range(2):
        for part in range(2):
            out[0, b, part] = ls[b, part] + ss[1 - b, part]

    @pl.when(has_left)
    def _():
        side_right().wait_recv()
        for part in range(2):
            out[0, 0, part] = out[0, 0, part] + sin[0, part]

    @pl.when(has_right)
    def _():
        side_left().wait_recv()
        for part in range(2):
            out[0, 1, part] = out[0, 1, part] + sin[1, part]

    @pl.when(has_right)
    def _():
        side_right().wait_send()

        @pl.when((s > 0) | (core == 1))
        def _():
            left_copy().wait_send()

    @pl.when(has_left)
    def _():
        side_left().wait_send()

        @pl.when((s < 3) | (core == 1))
        def _():
            right_copy().wait_send()

    for b in range(2):
        for part in range(2):
            own_copy(b, part).wait_send()

            @pl.when(has_p)
            def _():
                y_copy(True, b, part).wait_send()

            @pl.when(has_m)
            def _():
                y_copy(False, b, part).wait_send()

            @pl.when(((core == 0) & has_p) | ((core == 1) & has_m))
            def _():
                fwd_copy(hp, b, part).wait_send()


def local(onsite, hopping, coupling, broadening, born_sigma, phonon_shift, phonon_local, phonon_side):
    vmem = pl.BlockSpec(memory_space=pltpu.VMEM)
    smem = pl.BlockSpec(memory_space=pltpu.SMEM)
    dma = pltpu.SemaphoreType.DMA
    block = (2, N, N)
    pair = (2, 2, N, N)
    return pl.pallas_call(
        kernel,
        out_shape=jax.ShapeDtypeStruct(born_sigma.shape, F32),
        in_specs=[vmem, vmem, vmem, smem, vmem, smem, vmem, vmem],
        out_specs=vmem,
        scratch_shapes=[
            pltpu.VMEM(pair, F32),
            pltpu.VMEM((2, 4, N, N), BF16),
            pltpu.VMEM((7,) + block, F32),
            pltpu.VMEM((4,) + block, F32),
            pltpu.VMEM(pair, F32),
            pltpu.VMEM(pair, F32),
            pltpu.VMEM(pair, F32),
            pltpu.VMEM(pair, F32),
            pltpu.VMEM((5, N, N), F32),
            pltpu.VMEM((5, N, N), F32),
            pltpu.VMEM(pair, F32),
            pltpu.VMEM(pair, F32),
            pltpu.VMEM(pair, F32),
            dma((2,)), dma((2,)),
            dma((2, 2, 2)), dma((2, 2, 2)),
            dma((2, 2)), dma((2, 2)),
            dma((2, 2)), dma((2, 2)),
            dma((2,)), dma((2,)),
            pltpu.SemaphoreType.REGULAR,
        ],
        compiler_params=pltpu.CompilerParams(
            collective_id=0, has_side_effects=True, vmem_limit_bytes=56 * 2**20
        ),
        cost_estimate=pl.CostEstimate(flops=6 * 60 * 2 * N**3, bytes_accessed=6 * 2**20, transcendentals=0),
    )(onsite, hopping, coupling, broadening, born_sigma, phonon_shift, phonon_local, phonon_side)


def solution(mesh):
    in_specs = (
        P("section", None),
        P("section", None, None),
        P("section", None, None),
        P("energy"),
        P("energy", "section", None, None, None),
        P(),
        P(),
        P(),
    )
    out_specs = P("energy", "section", None, None, None)
    return jax.shard_map(local, mesh=mesh, in_specs=in_specs, out_specs=out_specs, check_vma=False)
```

profile of v0, /device:TPU:96, one launch (start us, length us, event | category | flops | bytes accessed | tf_op | source)
XLA Modules:
  0.0 83.3 jit_solution(7387118185743004118)
XLA Ops:
  0.7 80.4 %shard_map.82 = f32[1,2,2,256,256]{4,3,2,1,0:T(8,128)} custom-call(f32[2,256]{1,0:T(2,128)} %onsite.1, f32[2,256,256]{2,1,0:T(8,128)} %hop.1, f32[2,256,256]{2,1,0:T(8,128)} %coup.1, f32[1]{0:T(128)S(6)} %copy.10.broad, f32[1,2,2,256,256]{4,3,2,1,0:T(8,128)} %born.1, s32[4]{0:T(128)} %shift.1, f32[4,256,256]{2,1,0:T(8,128)} %ploc.1, f32[4,256,256]{2,1,0:T(8,128)} %pside.1), custom_call_target="tpu_custom_call" | custom-call | flops 12079595520 | bytes 6291456 | tf_op jit(solution)/shard_map/pallas_call | solution.py:394
  81.0 2.3 %copy.11 = f32[1,2,2,256,256]{4,3,2,1,0:T(8,128)} copy(f32[1,2,2,256,256]{4,3,2,1,0:T(8,128)} %shard_map.82) | data formatting | bytes 2097152
where the time goes:
time: 84.6 us; the launch traced here: 83.3 us
  Pallas kernels  80.4 us (95%)
  local copies, waits for them, and re-layouts  2.29 us (3%)
    pallas_call x1, Pallas kernels, local(): pl.pallas_call(kernel, out_shape=jax.ShapeDtypeStruct(born_sigma.shape, F...  80.4 us
    unnamed x1, local copies, waits for them, and re-layouts  2.29 us

commit v1 on v0

--- a/solution.py
+++ b/solution.py
@@ -99,6 +99,7 @@
     has_m = e >= 2
     has_right = s < 3
     has_left = s > 0
+    early = jnp.where(s < 2, 1, 0)
 
     barrier = pltpu.get_barrier_semaphore()
 
@@ -134,14 +135,26 @@
     def own_copy(b, part):
         return remote(green.at[b, part], ho.at[b, part], o_s.at[b, part], o_r.at[b, part], {"energy": other})
 
+    def send_block(b):
+        for part in range(2):
+            @pl.when(has_p)
+            def _():
+                y_copy(True, b, part).start()
+
+            @pl.when(has_m)
+            def _():
+                y_copy(False, b, part).start()
+
     def fwd_copy(src, b, part):
         return remote(src.at[b, part], hf.at[b, part], f_s.at[b, part], f_r.at[b, part], {"energy": other})
 
-    def side_right():
-        return remote(ss.at[1], sin.at[0], side_s.at[1], side_r.at[0], {"section": lax.rem(s + 1, 4)})
-
-    def side_left():
-        return remote(ss.at[0], sin.at[1], side_s.at[0], side_r.at[1], {"section": lax.rem(s + 3, 4)})
+    def side_right(part):
+        return remote(ss.at[1, part], sin.at[0, part], side_s.at[1, part], side_r.at[0, part],
+                      {"section": lax.rem(s + 1, 4)})
+
+    def side_left(part):
+        return remote(ss.at[0, part], sin.at[1, part], side_s.at[0, part], side_r.at[1, part],
+                      {"section": lax.rem(s + 3, 4)})
 
     energy = -2.0 + 4.0 * e.astype(F32) / 31.0
     eta = broad[0]
@@ -266,25 +279,24 @@
             @pl.when(kind == 3)
             def _():
                 for part in range(2):
-                    @pl.when(has_p)
-                    def _():
-                        y_copy(True, b, part).start()
-
-                    @pl.when(has_m)
-                    def _():
-                        y_copy(False, b, part).start()
-
                     own_copy(b, part).start()
 
+                @pl.when(b == early)
+                def _():
+                    send_block(b)
+
         return code // 8
 
     lax.fori_loop(0, SLOTS, slot, at_section([order_code(d) for d in ORDERS]))
 
     def units(t, carry):
-        first = jnp.where(s < 2, 1, 0)
         half = t // 2
-        b = first + half - 2 * first * half
+        b = early + half - 2 * early * half
         part = lax.rem(t, 2)
+
+        @pl.when(t == 0)
+        def _():
+            send_block(1 - early)
 
         def add(source, d):
             x = source[b, part]
@@ -322,15 +334,13 @@
             fwd_copy(hp, b, part).wait_recv()
             add(hf, 1 + 2 * core)
 
-        @pl.when(part == 1)
-        def _():
-            @pl.when((b == 1) & has_right)
-            def _():
-                side_right().start()
-
-            @pl.when((b == 0) & has_left)
-            def _():
-                side_left().start()
+        @pl.when((b == 1) & has_right)
+        def _():
+            side_right(part).start()
+
+        @pl.when((b == 0) & has_left)
+        def _():
+            side_left(part).start()
 
         return carry
 
@@ -342,19 +352,20 @@
 
     @pl.when(has_left)
     def _():
-        side_right().wait_recv()
-        for part in range(2):
+        for part in range(2):
+            side_right(part).wait_recv()
             out[0, 0, part] = out[0, 0, part] + sin[0, part]
 
     @pl.when(has_right)
     def _():
-        side_left().wait_recv()
-        for part in range(2):
+        for part in range(2):
+            side_left(part).wait_recv()
             out[0, 1, part] = out[0, 1, part] + sin[1, part]
 
     @pl.when(has_right)
     def _():
-        side_right().wait_send()
+        for part in range(2):
+            side_right(part).wait_send()
 
         @pl.when((s > 0) | (core == 1))
         def _():
@@ -362,7 +373,8 @@
 
     @pl.when(has_left)
     def _():
-        side_left().wait_send()
+        for part in range(2):
+            side_left(part).wait_send()
 
         @pl.when((s < 3) | (core == 1))
         def _():
@@ -414,7 +426,7 @@
             dma((2, 2, 2)), dma((2, 2, 2)),
             dma((2, 2)), dma((2, 2)),
             dma((2, 2)), dma((2, 2)),
-            dma((2,)), dma((2,)),
+            dma((2, 2)), dma((2, 2)),
             pltpu.SemaphoreType.REGULAR,
         ],
         compiler_params=pltpu.CompilerParams(

time: 84.6 us -> 79.7 us (0.942); the launches traced: 83.3 us -> 79.5 us
  Pallas kernels: 80.4 us -> 76.5 us
    pallas_call x1, Pallas kernels: 80.4 us -> 76.5 us  [local(): pl.pallas_call(kernel, out_shape=jax.ShapeDtypeStruct(born_sigma.shape, F...]
where the time goes in v1:
time: 79.7 us; the launch traced here: 79.5 us
  Pallas kernels  76.5 us (96%)
  local copies, waits for them, and re-layouts  2.29 us (3%)
    pallas_call x1, Pallas kernels, local(): pl.pallas_call(kernel, out_shape=jax.ShapeDtypeStruct(born_sigma.shape, F...  76.5 us
    unnamed x1, local copies, waits for them, and re-layouts  2.29 us

profile of v1, /device:TPU:96, one launch (start us, length us, event | category | flops | bytes accessed | tf_op | source)
XLA Modules:
  0.0 79.5 jit_solution(10524368525523496802)
XLA Ops:
  0.7 76.5 %shard_map.82 = f32[1,2,2,256,256]{4,3,2,1,0:T(8,128)} custom-call(f32[2,256]{1,0:T(2,128)} %onsite.1, f32[2,256,256]{2,1,0:T(8,128)} %hop.1, f32[2,256,256]{2,1,0:T(8,128)} %coup.1, f32[1]{0:T(128)S(6)} %copy.10.broad, f32[1,2,2,256,256]{4,3,2,1,0:T(8,128)} %born.1, s32[4]{0:T(128)} %shift.1, f32[4,256,256]{2,1,0:T(8,128)} %ploc.1, f32[4,256,256]{2,1,0:T(8,128)} %pside.1), custom_call_target="tpu_custom_call" | custom-call | flops 12079595520 | bytes 6291456 | tf_op jit(solution)/shard_map/pallas_call | solution.py:406
  77.2 2.3 %copy.11 = f32[1,2,2,256,256]{4,3,2,1,0:T(8,128)} copy(f32[1,2,2,256,256]{4,3,2,1,0:T(8,128)} %shard_map.82) | data formatting | bytes 2097152

commit v2 on v1

v2 whole, which is shorter than its diff:
```python
import jax
import jax.numpy as jnp
from jax import lax
from jax.experimental import pallas as pl
from jax.experimental.pallas import tpu as pltpu
from jax.sharding import PartitionSpec as P

MODES = 4
N = 256
F32 = jnp.float32
BF16 = jnp.bfloat16
MESH = pl.DeviceIdType.MESH

L, R, G = 4, 8, 12
ORDERS = (
    ((L, L + 1, G + 1, R + 1, G), (L, L + 1, L + 2, L + 3, G + 1, R + 1, G),
     (R + 1, R, R + 3, R + 2, G, L, G + 1), (R + 1, R, G, L, G + 1)),
    ((L, L + 1, G + 1, R + 1, G), (L, L + 1, R + 1, R, G + 1, G),
     (R + 1, R, L, L + 1, G, G + 1), (R + 1, R, G, L, G + 1)),
)
SLOTS = 7
CUTS = 1
UNITS = 2 * CUTS
ROWS = N // CUTS


def order_code(steps):
    return sum(step * 16**i for i, step in enumerate(steps))


def cat(parts, axis):
    return jnp.concatenate(parts, axis=axis)


def split(x):
    hi = x.astype(BF16)
    return hi, (x - hi.astype(F32)).astype(BF16)


def dot3(a, b):
    return jnp.dot(
        cat([a[0], a[1], a[0]], 1), cat([b[0], b[0], b[1]], 0), preferred_element_type=F32
    )


def halves(re, im):
    return split(re), split(im), split(re + im)


def cdot(a, b):
    p1 = dot3(a[0], b[0])
    p2 = dot3(a[1], b[1])
    p3 = dot3(a[2], b[2])
    return p1 - p2, p3 - p1 - p2


def diagonal_mask():
    return lax.broadcasted_iota(jnp.int32, (N, N), 0) == lax.broadcasted_iota(jnp.int32, (N, N), 1)


def inverse(mr, mi):
    eye = diagonal_mask()

    def reciprocal(axis):
        dr = jnp.sum(jnp.where(eye, mr, 0.0), axis=axis, keepdims=True)
        di = jnp.sum(jnp.where(eye, mi, 0.0), axis=axis, keepdims=True)
        modulus = dr * dr + di * di
        return dr / modulus, -di / modulus

    xr, xi = reciprocal(0)
    rr = jnp.where(eye, 0.0, mi * xi - mr * xr)
    ri = jnp.where(eye, 0.0, -(mr * xi + mi * xr))
    r = halves(rr, ri)
    sr, si = cdot(r, r)
    s = halves(sr, si)
    tr, ti = cdot(s, s)
    ur, ui = cdot(r, s)
    yr = jnp.where(eye, 1.0, rr) + sr + ur
    yi = ri + si + ui
    ur, ui = cdot(halves(yr, yi), halves(tr, ti))
    yr = yr + ur
    yi = yi + ui
    cr, ci = reciprocal(1)
    return yr * cr - yi * ci, yr * ci + yi * cr


def couple(a, gr, gi, b):
    gr, gi = split(gr), split(gi)
    g = (cat([gr[0], gi[0]], 1), cat([gr[1], gi[1]], 1))
    hi, lo = split(dot3(a, g))
    hi = cat([hi[:, :N], hi[:, N:]], 0)
    lo = cat([lo[:, :N], lo[:, N:]], 0)
    both = dot3((hi, lo), b)
    return both[:N], both[N:]


def kernel(
    onsite, hop, coup, broad, born, shift, ploc, pside, out,
    system, links, sig, green, late, hp, hm, ho, hf, wl, ws, ls, ss, sin, fcoup,
    chain_s, chain_r, y_s, y_r, o_s, o_r, f_s, f_r, side_s, side_r, pre_s, pre_r, go,
):
    e = lax.axis_index("energy")
    s = lax.axis_index("section")
    core = lax.rem(e, 2)
    other = e + 1 - 2 * core
    has_p = e < 30
    has_m = e >= 2
    has_right = s < 3
    has_left = s > 0
    middle = (s == 1) | (s == 2)
    early = jnp.where(s < 2, 1, 0)

    barrier = pltpu.get_barrier_semaphore()

    def greet(cond, where):
        @pl.when(cond)
        def _():
            pl.semaphore_signal(barrier, inc=1, device_id=where, device_id_type=MESH)

    for distance in (1, 2, 3):
        pl.semaphore_signal(
            barrier, inc=1, device_id={"section": lax.rem(s + distance, 4)}, device_id_type=MESH
        )
    greet(has_p, {"energy": lax.rem(e + 2, 32)})
    greet(has_m, {"energy": lax.rem(e + 30, 32)})
    pl.semaphore_signal(barrier, inc=1, device_id={"energy": other}, device_id_type=MESH)

    def remote(src, dst, ssem, rsem, where):
        return pltpu.make_async_remote_copy(
            src_ref=src, dst_ref=dst, send_sem=ssem, recv_sem=rsem, device_id=where, device_id_type=MESH
        )

    def left_copy():
        return remote(sig.at[5], sig.at[1], chain_s.at[0], chain_r.at[0], {"section": lax.rem(s + 1, 4)})

    def right_copy():
        return remote(green.at[2], late.at[0], chain_s.at[1], chain_r.at[1], {"section": lax.rem(s + 3, 4)})

    def far_left_copy():
        return remote(sig.at[8], sig.at[1], chain_s.at[2], chain_r.at[0], {"section": lax.rem(s + 2, 4)})

    def far_right_copy():
        return remote(green.at[4], late.at[0], chain_s.at[2], chain_r.at[1], {"section": lax.rem(s + 2, 4)})

    swap = {"section": lax.rem(7 - s, 4)}

    def system_copy(b):
        return remote(system.at[b], system.at[2 + b], pre_s.at[b], pre_r.at[b], swap)

    def coupling_copy():
        return remote(coup, fcoup, pre_s.at[2], pre_r.at[2], swap)

    def y_copy(up, b, part):
        if up:
            return remote(green.at[b, part], hm.at[b, part], y_s.at[0, b, part], y_r.at[0, b, part],
                          {"energy": lax.rem(e + 2, 32)})
        return remote(green.at[b, part], hp.at[b, part], y_s.at[1, b, part], y_r.at[1, b, part],
                      {"energy": lax.rem(e + 30, 32)})

    def own_copy(b, part):
        return remote(green.at[b, part], ho.at[b, part], o_s.at[b, part], o_r.at[b, part], {"energy": other})

    def send_block(b):
        for part in range(UNITS):
            @pl.when(has_p)
            def _():
                y_copy(True, b, part).start()

            @pl.when(has_m)
            def _():
                y_copy(False, b, part).start()

    def fwd_copy(src, b, part):
        return remote(src.at[b, part], hf.at[b, part], f_s.at[b, part], f_r.at[b, part], {"energy": other})

    def side_right(part):
        return remote(ss.at[1, part], sin.at[0, part], side_s.at[1, part], side_r.at[0, part],
                      {"section": lax.rem(s + 1, 4)})

    def side_left(part):
        return remote(ss.at[0, part], sin.at[1, part], side_s.at[0, part], side_r.at[1, part],
                      {"section": lax.rem(s + 3, 4)})

    energy = -2.0 + 4.0 * e.astype(F32) / 31.0
    eta = broad[0]

    def link_halves(v, place):
        vh, vl = split(v)
        links[place, 0] = vh
        links[place, 1] = vl
        vh, vl = split(v.T)
        links[place, 2] = vh
        links[place, 3] = vl

    def setup(b, carry):
        eye = diagonal_mask()
        h = hop[b]
        ham = 0.5 * (h + h.T)
        system[b, 0] = jnp.where(eye, energy - onsite[pl.ds(b, 1), :], 0.0) - ham - born[0, b, 0]
        system[b, 1] = jnp.where(eye, eta, 0.0) - born[0, b, 1]
        link_halves(coup[b], b)
        return carry

    lax.fori_loop(0, 2, setup, 0)
    sig[0] = jnp.zeros((2, N, N), F32)

    @pl.when(s == 0)
    def _():
        sig[1] = jnp.zeros((2, N, N), F32)

    @pl.when(s == 3)
    def _():
        sig[4] = jnp.zeros((2, N, N), F32)

    def everyone_is_in():
        pl.semaphore_wait(barrier, 4 + has_p.astype(jnp.int32) + has_m.astype(jnp.int32))

    def weights():
        def one(d, carry):
            wloc = jnp.zeros((N, N), F32)
            wside = jnp.zeros((N, N), F32)
            for k in range(MODES):
                on = jnp.where(shift[k] == d - 2, 1.0, 0.0)
                wloc = wloc + on * ploc[k]
                wside = wside + on * pside[k]
            wl[d] = wloc.reshape(CUTS, ROWS, N)
            ws[d] = wside.reshape(CUTS, ROWS, N)
            return carry

        lax.fori_loop(0, 5, one, 0)

    first_block = lax.rem(s, 2)
    last_block = 1 - first_block

    @pl.when(middle)
    def _():
        everyone_is_in()

    @pl.when(middle & (core == 0))
    def _():
        coupling_copy().start()
        system_copy(first_block).start()

    @pl.when(middle)
    def _():
        weights()

    @pl.when(middle & (core == 0))
    def _():
        coupling_copy().wait_recv()

        def foreign(b, carry):
            link_halves(fcoup[b], 2 + b)
            return carry

        lax.fori_loop(0, 2, foreign, 0)
        coupling_copy().wait_send()
        system_copy(last_block).start()

    def pick(b, values):
        return jnp.where(b == 0, values[0], jnp.where(b == 1, values[1], jnp.where(b == 2, values[2], values[3])))

    def slot(i, code):
        digit = lax.rem(code, 16)
        kind = digit // 4
        b = lax.rem(digit, 4)
        is_l = kind == 1
        is_r = kind == 2

        @pl.when((i == 2) & jnp.logical_not(middle))
        def _():
            weights()

        @pl.when(i == pick(s, (9, 0, 4 - 2 * core, 2)))
        def _():
            left_copy().wait_recv()

        @pl.when(i == pick(s, (2, 4 - 2 * core, 0, 9)))
        def _():
            right_copy().wait_recv()
            re, im = couple((links[1, 0], links[1, 1]), late[0, :CUTS].reshape(N, N), late[0, CUTS:].reshape(N, N), (links[1, 2], links[1, 3]))
            sig[4, 0] = re
            sig[4, 1] = im

        @pl.when(kind > 0)
        def _():
            @pl.when(b >= 2)
            def _():
                system_copy(b - 2).wait_recv()

            first = jnp.where(is_r, 0, pick(b, (1, 2, 5, 7)))
            second = jnp.where(is_l, 0, pick(b, (3, 4, 8, 7)))
            place = jnp.where(kind == 3, b, jnp.where(is_r, pick(b, (2, 3, 4, 3)), 3))
            re, im = inverse(
                system[b, 0] - sig[first, 0] - sig[second, 0], system[b, 1] - sig[first, 1] - sig[second, 1]
            )
            green[place, :CUTS] = re.reshape(CUTS, ROWS, N)
            green[place, CUTS:] = im.reshape(CUTS, ROWS, N)

            at_end = (i == 1) & jnp.logical_not(middle)

            @pl.when(at_end)
            def _():
                everyone_is_in()

            @pl.when(at_end & (s == 3) & (core == 1))
            def _():
                pl.semaphore_wait(go, 1)

            @pl.when(is_r & (b == 0))
            def _():
                right_copy().start()

            @pl.when(is_r & (b == 2))
            def _():
                far_right_copy().start()

            @pl.when(is_l | (is_r & ((b == 1) | (b == 3) | ((b == 0) & (s == 2) & (core == 0)))))
            def _():
                v = jnp.where(is_l, b, pick(b, (3, 0, 0, 2)))
                a0 = jnp.where(is_l, 2, 0)
                b0 = 2 - a0
                target = jnp.where(is_l, pick(b, (2, 5, 7, 8)), pick(b, (7, 3, 0, 8)))
                re, im = couple((links[v, a0], links[v, a0 + 1]), green[place, :CUTS].reshape(N, N), green[place, CUTS:].reshape(N, N),
                                (links[v, b0], links[v, b0 + 1]))
                sig[target, 0] = re
                sig[target, 1] = im

            @pl.when(at_end & (s == 0) & (core == 1))
            def _():
                pl.semaphore_wait(go, 1)

            @pl.when(is_l & (b == 1))
            def _():
                left_copy().start()

            @pl.when(is_l & (b == 3))
            def _():
                far_left_copy().start()

            @pl.when(at_end & (core == 0))
            def _():
                @pl.when(s == 0)
                def _():
                    left_copy().wait_send()

                @pl.when(s == 3)
                def _():
                    right_copy().wait_send()

                pl.semaphore_signal(go, inc=1, device_id={"energy": other}, device_id_type=MESH)

            @pl.when(kind == 3)
            def _():
                for part in range(UNITS):
                    own_copy(b, part).start()

                @pl.when(b == early)
                def _():
                    send_block(b)

        return code // 16

    codes = [pick(s, [order_code(x) for x in orders]) for orders in ORDERS]
    lax.fori_loop(0, SLOTS, slot, jnp.where(core == 0, codes[0], codes[1]))

    def units(t, carry):
        half = t // UNITS
        b = early + half - 2 * early * half
        part = lax.rem(t, UNITS)
        rows = lax.rem(t, CUTS)

        @pl.when(t == 0)
        def _():
            send_block(1 - early)

        def add(source, d):
            x = source[b, part]
            ls[b, part] = ls[b, part] + wl[d, rows] * x
            ss[b, part] = ss[b, part] + ws[d, rows] * x

        x = green[b, part]
        ls[b, part] = wl[2, rows] * x
        ss[b, part] = ws[2, rows] * x
        own_copy(b, part).wait_recv()
        add(ho, 3 - 2 * core)

        @pl.when(has_p)
        def _():
            y_copy(False, b, part).wait_recv()

            @pl.when(core == 0)
            def _():
                fwd_copy(hp, b, part).start()

            add(hp, 4)

        @pl.when(has_m)
        def _():
            y_copy(True, b, part).wait_recv()

            @pl.when(core == 1)
            def _():
                fwd_copy(hm, b, part).start()

            add(hm, 0)

        @pl.when(((core == 0) & has_m) | ((core == 1) & has_p))
        def _():
            fwd_copy(hp, b, part).wait_recv()
            add(hf, 1 + 2 * core)

        @pl.when((b == 1) & has_right)
        def _():
            side_right(part).start()

        @pl.when((b == 0) & has_left)
        def _():
            side_left(part).start()

        return carry

    lax.fori_loop(0, 2 * UNITS, units, 0)

    def finish(t, carry):
        b = t // UNITS
        part = lax.rem(t, UNITS)

        @pl.when((b == 0) & has_left)
        def _():
            side_right(part).wait_recv()

        @pl.when((b == 1) & has_right)
        def _():
            side_left(part).wait_recv()

        away = jnp.where(jnp.where(b == 0, has_left, has_right), sin[b, part], 0.0)
        rows = pl.ds(pl.multiple_of(lax.rem(t, CUTS) * ROWS, ROWS), ROWS)
        out[0, b, part // CUTS, rows, :] = ls[b, part] + ss[1 - b, part] + away
        return carry

    lax.fori_loop(0, 2 * UNITS, finish, 0)

    @pl.when(has_right)
    def _():
        for part in range(UNITS):
            side_right(part).wait_send()

        @pl.when((s == 1) | (core == 1))
        def _():
            left_copy().wait_send()

    @pl.when(has_left)
    def _():
        for part in range(UNITS):
            side_left(part).wait_send()

        @pl.when((s == 2) | (core == 1))
        def _():
            right_copy().wait_send()

    @pl.when(middle & (core == 0))
    def _():
        far_left_copy().wait_send()
        system_copy(first_block).wait_send()
        system_copy(last_block).wait_send()

    for b in range(2):
        for part in range(UNITS):
            own_copy(b, part).wait_send()

            @pl.when(has_p)
            def _():
                y_copy(True, b, part).wait_send()

            @pl.when(has_m)
            def _():
                y_copy(False, b, part).wait_send()

            @pl.when(((core == 0) & has_p) | ((core == 1) & has_m))
            def _():
                fwd_copy(hp, b, part).wait_send()


def local(onsite, hopping, coupling, broadening, born_sigma, phonon_shift, phonon_local, phonon_side):
    vmem = pl.BlockSpec(memory_space=pltpu.VMEM)
    smem = pl.BlockSpec(memory_space=pltpu.SMEM)
    dma = pltpu.SemaphoreType.DMA
    block = (2, N, N)
    pieces = (UNITS, ROWS, N)
    return pl.pallas_call(
        kernel,
        out_shape=jax.ShapeDtypeStruct(born_sigma.shape, F32),
        in_specs=[vmem, vmem, vmem, smem, vmem, smem, vmem, vmem],
        out_specs=vmem,
        scratch_shapes=[
            pltpu.VMEM((4,) + block, F32),
            pltpu.VMEM((4, 4, N, N), BF16),
            pltpu.VMEM((9,) + block, F32),
            pltpu.VMEM((5,) + pieces, F32),
            pltpu.VMEM((1,) + pieces, F32),
            pltpu.VMEM((2,) + pieces, F32),
            pltpu.VMEM((2,) + pieces, F32),
            pltpu.VMEM((2,) + pieces, F32),
            pltpu.VMEM((2,) + pieces, F32),
            pltpu.VMEM((5, CUTS, ROWS, N), F32),
            pltpu.VMEM((5, CUTS, ROWS, N), F32),
            pltpu.VMEM((2,) + pieces, F32),
            pltpu.VMEM((2,) + pieces, F32),
            pltpu.VMEM((2,) + pieces, F32),
            pltpu.VMEM(block, F32),
            dma((3,)), dma((2,)),
            dma((2, 2, UNITS)), dma((2, 2, UNITS)),
            dma((2, UNITS)), dma((2, UNITS)),
            dma((2, UNITS)), dma((2, UNITS)),
            dma((2, UNITS)), dma((2, UNITS)),
            dma((3,)), dma((3,)),
            pltpu.SemaphoreType.REGULAR,
        ],
        compiler_params=pltpu.CompilerParams(
            collective_id=0, has_side_effects=True, vmem_limit_bytes=56 * 2**20
        ),
        cost_estimate=pl.CostEstimate(flops=6 * 60 * 2 * N**3, bytes_accessed=6 * 2**20, transcendentals=0),
    )(onsite, hopping, coupling, broadening, born_sigma, phonon_shift, phonon_local, phonon_side)


def solution(mesh):
    in_specs = (
        P("section", None),
        P("section", None, None),
        P("section", None, None),
        P("energy"),
        P("energy", "section", None, None, None),
        P(),
        P(),
        P(),
    )
    out_specs = P("energy", "section", None, None, None)
    return jax.shard_map(local, mesh=mesh, in_specs=in_specs, out_specs=out_specs, check_vma=False)
```

time: 79.7 us -> 75 us (0.941)
  Pallas kernels: 76.5 us -> 71.1 us
    pallas_call x1, Pallas kernels: 76.5 us -> 71.1 us  [local(): pl.pallas_call(kernel, out_shape=jax.ShapeDtypeStruct(born_sigma.shape, F...]
where the time goes in v2:
time: 75 us; the launch traced here: 74 us
  Pallas kernels  71.1 us (95%)
  local copies, waits for them, and re-layouts  2.29 us (3%)
    pallas_call x1, Pallas kernels, local(): pl.pallas_call(kernel, out_shape=jax.ShapeDtypeStruct(born_sigma.shape, F...  71.1 us
    unnamed x1, local copies, waits for them, and re-layouts  2.29 us

profile of v2, /device:TPU:96, one launch (start us, length us, event | category | flops | bytes accessed | tf_op | source)
XLA Modules:
  0.0 74.0 jit_solution(9763517696013915638)
XLA Ops:
  0.7 71.1 %shard_map.82 = f32[1,2,2,256,256]{4,3,2,1,0:T(8,128)} custom-call(f32[2,256]{1,0:T(2,128)} %onsite.1, f32[2,256,256]{2,1,0:T(8,128)} %hop.1, f32[2,256,256]{2,1,0:T(8,128)} %coup.1, f32[1]{0:T(128)S(6)} %copy.10.broad, f32[1,2,2,256,256]{4,3,2,1,0:T(8,128)} %born.1, s32[4]{0:T(128)} %shift.1, f32[4,256,256]{2,1,0:T(8,128)} %ploc.1, f32[4,256,256]{2,1,0:T(8,128)} %pside.1), custom_call_target="tpu_custom_call" | custom-call | flops 12079595520 | bytes 6291456 | tf_op jit(solution)/shard_map/pallas_call | solution.py:491
  71.8 2.3 %copy.11 = f32[1,2,2,256,256]{4,3,2,1,0:T(8,128)} copy(f32[1,2,2,256,256]{4,3,2,1,0:T(8,128)} %shard_map.82) | data formatting | bytes 2097152

commit v3 on v2

--- a/solution.py
+++ b/solution.py
@@ -95,7 +95,8 @@
 
 
 def kernel(
-    onsite, hop, coup, broad, born, shift, ploc, pside, out,
+    onsite, hop_in, coup_in, broad, born_in, shift, ploc_in, pside_in, out,
+    hop, coup, born, ploc, pside, load,
     system, links, sig, green, late, hp, hm, ho, hf, wl, ws, ls, ss, sin, fcoup,
     chain_s, chain_r, y_s, y_r, o_s, o_r, f_s, f_r, side_s, side_r, pre_s, pre_r, go,
 ):
@@ -110,6 +111,26 @@
     middle = (s == 1) | (s == 2)
     early = jnp.where(s < 2, 1, 0)
 
+    opening = jnp.where(s < 2, 0, 1)
+
+    def loads(b):
+        return [
+            pltpu.make_async_copy(source.at[b], target.at[b], load.at[3 * b + k])
+            for k, (source, target) in enumerate(((hop_in, hop), (born_in.at[0], born), (coup_in, coup)))
+        ]
+
+    def phonon_loads():
+        return [
+            pltpu.make_async_copy(ploc_in, ploc, load.at[6]),
+            pltpu.make_async_copy(pside_in, pside, load.at[7]),
+        ]
+
+    for b in (opening, 1 - opening):
+        for copy in loads(b):
+            copy.start()
+    for copy in phonon_loads():
+        copy.start()
+
     barrier = pltpu.get_barrier_semaphore()
 
     def greet(cond, where):
@@ -192,12 +213,15 @@
         links[place, 2] = vh
         links[place, 3] = vl
 
-    def setup(b, carry):
+    def setup(t, carry):
+        b = opening + t - 2 * opening * t
+        for copy in loads(b):
+            copy.wait()
         eye = diagonal_mask()
         h = hop[b]
         ham = 0.5 * (h + h.T)
-        system[b, 0] = jnp.where(eye, energy - onsite[pl.ds(b, 1), :], 0.0) - ham - born[0, b, 0]
-        system[b, 1] = jnp.where(eye, eta, 0.0) - born[0, b, 1]
+        system[b, 0] = jnp.where(eye, energy - onsite[pl.ds(b, 1), :], 0.0) - ham - born[b, 0]
+        system[b, 1] = jnp.where(eye, eta, 0.0) - born[b, 1]
         link_halves(coup[b], b)
         return carry
 
@@ -216,6 +240,9 @@
         pl.semaphore_wait(barrier, 4 + has_p.astype(jnp.int32) + has_m.astype(jnp.int32))
 
     def weights():
+        for copy in phonon_loads():
+            copy.wait()
+
         def one(d, carry):
             wloc = jnp.zeros((N, N), F32)
             wside = jnp.zeros((N, N), F32)
@@ -485,15 +512,22 @@
 def local(onsite, hopping, coupling, broadening, born_sigma, phonon_shift, phonon_local, phonon_side):
     vmem = pl.BlockSpec(memory_space=pltpu.VMEM)
     smem = pl.BlockSpec(memory_space=pltpu.SMEM)
+    hbm = pl.BlockSpec(memory_space=pl.ANY)
     dma = pltpu.SemaphoreType.DMA
     block = (2, N, N)
     pieces = (UNITS, ROWS, N)
     return pl.pallas_call(
         kernel,
-        out_shape=jax.ShapeDtypeStruct(born_sigma.shape, F32),
-        in_specs=[vmem, vmem, vmem, smem, vmem, smem, vmem, vmem],
+        out_shape=pltpu.VMEM(born_sigma.shape, F32),
+        in_specs=[vmem, hbm, hbm, smem, hbm, smem, hbm, hbm],
         out_specs=vmem,
         scratch_shapes=[
+            pltpu.VMEM((2, N, N), F32),
+            pltpu.VMEM((2, N, N), F32),
+            pltpu.VMEM((2, 2, N, N), F32),
+            pltpu.VMEM((MODES, N, N), F32),
+            pltpu.VMEM((MODES, N, N), F32),
+            dma((8,)),
             pltpu.VMEM((4,) + block, F32),
             pltpu.VMEM((4, 4, N, N), BF16),
             pltpu.VMEM((9,) + block, F32),

time: 75 us -> 72.6 us (0.968)
  local copies, waits for them, and re-layouts: 2.29 us -> 0.97 us
  Pallas kernels: 71.1 us -> 70 us
    unnamed x1, local copies, waits for them, and re-layouts: 2.29 us -> 0.97 us
    pallas_call x1, Pallas kernels: 71.1 us -> 70 us  [local(): pl.pallas_call(kernel, out_shape=pltpu.VMEM(born_sigma.shape, F32), in_sp...]
where the time goes in v3:
time: 72.6 us; the launch traced here: 71.7 us
  Pallas kernels  70 us (96%)
  local copies, waits for them, and re-layouts  0.97 us (1%)
    pallas_call x1, Pallas kernels, local(): pl.pallas_call(kernel, out_shape=pltpu.VMEM(born_sigma.shape, F32), in_sp...  70 us

profile of v3, /device:TPU:96, one launch (start us, length us, event | category | flops | bytes accessed | tf_op | source)
XLA Modules:
  0.0 71.7 jit_solution(3233609212297453027)
XLA Ops:
  0.7 70.0 %shard_map.82 = f32[1,2,2,256,256]{4,3,2,1,0:T(8,128)S(1)} custom-call(f32[2,256]{1,0:T(2,128)} %onsite.1, f32[2,256,256]{2,1,0:T(8,128)} %hop_in.1, f32[2,256,256]{2,1,0:T(8,128)} %coup_in.1, f32[1]{0:T(128)S(6)} %copy.11.broad, f32[1,2,2,256,256]{4,3,2,1,0:T(8,128)} %born_in.1, s32[4]{0:T(128)} %shift.1, f32[4,256,256]{2,1,0:T(8,128)} %ploc_in.1, ...), custom_call_target="tpu_custom_call" | custom-call | flops 12079595520 | bytes 6291456 | tf_op jit(solution)/shard_map/pallas_call | solution.py:519
  70.7 1.0 %copy.10 = f32[1,2,2,256,256]{4,3,2,1,0:T(8,128)} copy(f32[1,2,2,256,256]{4,3,2,1,0:T(8,128)S(1)} %shard_map.82) | data formatting | bytes 2097152

commit v4 on v3

--- a/solution.py
+++ b/solution.py
@@ -19,7 +19,7 @@
      (R + 1, R, L, L + 1, G, G + 1), (R + 1, R, G, L, G + 1)),
 )
 SLOTS = 7
-CUTS = 1
+CUTS = 2
 UNITS = 2 * CUTS
 ROWS = N // CUTS
 
@@ -401,41 +401,38 @@
         def _():
             send_block(1 - early)
 
-        def add(source, d):
-            x = source[b, part]
+        @pl.when(has_p)
+        def _():
+            y_copy(False, b, part).wait_recv()
+
+            @pl.when(core == 0)
+            def _():
+                fwd_copy(hp, b, part).start()
+
+        @pl.when(has_m)
+        def _():
+            y_copy(True, b, part).wait_recv()
+
+            @pl.when(core == 1)
+            def _():
+                fwd_copy(hm, b, part).start()
+
+        own_copy(b, part).wait_recv()
+        x = green[b, part]
+        near = ho[b, part]
+        up = jnp.where(has_p, hp[b, part], 0.0)
+        down = jnp.where(has_m, hm[b, part], 0.0)
+        d = 3 - 2 * core
+        ls[b, part] = wl[2, rows] * x + wl[d, rows] * near + wl[4, rows] * up + wl[0, rows] * down
+        ss[b, part] = ws[2, rows] * x + ws[d, rows] * near + ws[4, rows] * up + ws[0, rows] * down
+
+        @pl.when(((core == 0) & has_m) | ((core == 1) & has_p))
+        def _():
+            fwd_copy(hp, b, part).wait_recv()
+            x = hf[b, part]
+            d = 1 + 2 * core
+            ss[b, part] = ss[b, part] + ws[d, rows] * x
             ls[b, part] = ls[b, part] + wl[d, rows] * x
-            ss[b, part] = ss[b, part] + ws[d, rows] * x
-
-        x = green[b, part]
-        ls[b, part] = wl[2, rows] * x
-        ss[b, part] = ws[2, rows] * x
-        own_copy(b, part).wait_recv()
-        add(ho, 3 - 2 * core)
-
-        @pl.when(has_p)
-        def _():
-            y_copy(False, b, part).wait_recv()
-
-            @pl.when(core == 0)
-            def _():
-                fwd_copy(hp, b, part).start()
-
-            add(hp, 4)
-
-        @pl.when(has_m)
-        def _():
-            y_copy(True, b, part).wait_recv()
-
-            @pl.when(core == 1)
-            def _():
-                fwd_copy(hm, b, part).start()
-
-            add(hm, 0)
-
-        @pl.when(((core == 0) & has_m) | ((core == 1) & has_p))
-        def _():
-            fwd_copy(hp, b, part).wait_recv()
-            add(hf, 1 + 2 * core)
 
         @pl.when((b == 1) & has_right)
         def _():

time: 72.6 us -> 72.1 us (level)
  no operation moved by 1% of the time
where the time goes in v4:
time: 72.1 us; the launch traced here: 71.4 us
  Pallas kernels  69.8 us (97%)
  local copies, waits for them, and re-layouts  0.97 us (1%)
    pallas_call x1, Pallas kernels, local(): pl.pallas_call(kernel, out_shape=pltpu.VMEM(born_sigma.shape, F32), in_sp...  69.8 us

profile of v4, /device:TPU:96, one launch (start us, length us, event | category | flops | bytes accessed | tf_op | source)
XLA Modules:
  0.0 71.4 jit_solution(6495733645043135302)
XLA Ops:
  0.7 69.8 %shard_map.82 = f32[1,2,2,256,256]{4,3,2,1,0:T(8,128)S(1)} custom-call(f32[2,256]{1,0:T(2,128)} %onsite.1, f32[2,256,256]{2,1,0:T(8,128)} %hop_in.1, f32[2,256,256]{2,1,0:T(8,128)} %coup_in.1, f32[1]{0:T(128)S(6)} %copy.11.broad, f32[1,2,2,256,256]{4,3,2,1,0:T(8,128)} %born_in.1, s32[4]{0:T(128)} %shift.1, f32[4,256,256]{2,1,0:T(8,128)} %ploc_in.1, ...), custom_call_target="tpu_custom_call" | custom-call | flops 12079595520 | bytes 6291456 | tf_op jit(solution)/shard_map/pallas_call | solution.py:516
  70.4 1.0 %copy.10 = f32[1,2,2,256,256]{4,3,2,1,0:T(8,128)} copy(f32[1,2,2,256,256]{4,3,2,1,0:T(8,128)S(1)} %shard_map.82) | data formatting | bytes 2097152

commit v5 on v4

--- a/solution.py
+++ b/solution.py
@@ -38,9 +38,10 @@
 
 
 def dot3(a, b):
-    return jnp.dot(
-        cat([a[0], a[1], a[0]], 1), cat([b[0], b[0], b[1]], 0), preferred_element_type=F32
-    )
+    def dot(x, y):
+        return jnp.dot(x, y, preferred_element_type=F32)
+
+    return dot(a[0], b[0]) + dot(a[1], b[0]) + dot(a[0], b[1])
 
 
 def halves(re, im):
@@ -334,9 +335,19 @@
             def _():
                 pl.semaphore_wait(go, 1)
 
-            @pl.when(is_r & (b == 0))
+            held_back = middle & (core == 0)
+
+            @pl.when(is_r & (b == 0) & jnp.logical_not(held_back))
             def _():
                 right_copy().start()
+
+            @pl.when(held_back & (i == 2) & (s == 2))
+            def _():
+                right_copy().start()
+
+            @pl.when(held_back & (i == 2) & (s == 1))
+            def _():
+                left_copy().start()
 
             @pl.when(is_r & (b == 2))
             def _():
@@ -357,7 +368,7 @@
             def _():
                 pl.semaphore_wait(go, 1)
 
-            @pl.when(is_l & (b == 1))
+            @pl.when(is_l & (b == 1) & jnp.logical_not(held_back))
             def _():
                 left_copy().start()
 

time: 72.1 us -> 76.6 us (1.062)
  Pallas kernels: 69.8 us -> 74.8 us
    pallas_call x1, Pallas kernels: 69.8 us -> 74.8 us  [local(): pl.pallas_call(kernel, out_shape=pltpu.VMEM(born_sigma.shape, F32), in_sp...]
where the time goes in v5:
time: 76.6 us; the launch traced here: 76.4 us
  Pallas kernels  74.8 us (98%)
  local copies, waits for them, and re-layouts  0.97 us (1%)
    pallas_call x1, Pallas kernels, local(): pl.pallas_call(kernel, out_shape=pltpu.VMEM(born_sigma.shape, F32), in_sp...  74.8 us

profile of v5, /device:TPU:96, one launch (start us, length us, event | category | flops | bytes accessed | tf_op | source)
XLA Modules:
  0.0 76.4 jit_solution(15353941581087108861)
XLA Ops:
  0.7 74.8 %shard_map.82 = f32[1,2,2,256,256]{4,3,2,1,0:T(8,128)S(1)} custom-call(f32[2,256]{1,0:T(2,128)} %onsite.1, f32[2,256,256]{2,1,0:T(8,128)} %hop_in.1, f32[2,256,256]{2,1,0:T(8,128)} %coup_in.1, f32[1]{0:T(128)S(6)} %copy.11.broad, f32[1,2,2,256,256]{4,3,2,1,0:T(8,128)} %born_in.1, s32[4]{0:T(128)} %shift.1, f32[4,256,256]{2,1,0:T(8,128)} %ploc_in.1, ...), custom_call_target="tpu_custom_call" | custom-call | flops 12079595520 | bytes 6291456 | tf_op jit(solution)/shard_map/pallas_call | solution.py:527
  75.4 1.0 %copy.10 = f32[1,2,2,256,256]{4,3,2,1,0:T(8,128)} copy(f32[1,2,2,256,256]{4,3,2,1,0:T(8,128)S(1)} %shard_map.82) | data formatting | bytes 2097152

commit v6 on v4

--- a/solution.py
+++ b/solution.py
@@ -38,9 +38,10 @@
 
 
 def dot3(a, b):
-    return jnp.dot(
-        cat([a[0], a[1], a[0]], 1), cat([b[0], b[0], b[1]], 0), preferred_element_type=F32
-    )
+    def dot(x, y):
+        return jnp.dot(x, y, preferred_element_type=F32)
+
+    return dot(a[0], b[0]) + dot(a[1], b[0]) + dot(a[0], b[1])
 
 
 def halves(re, im):

time: 72.1 us -> 72.2 us (level)
  no operation moved by 1% of the time
where the time goes in v6:
time: 72.2 us; the launch traced here: 71.5 us
  Pallas kernels  69.8 us (97%)
  local copies, waits for them, and re-layouts  0.97 us (1%)
    pallas_call x1, Pallas kernels, local(): pl.pallas_call(kernel, out_shape=pltpu.VMEM(born_sigma.shape, F32), in_sp...  69.8 us

profile of v6, /device:TPU:96, one launch (start us, length us, event | category | flops | bytes accessed | tf_op | source)
XLA Modules:
  0.0 71.5 jit_solution(567375993647501091)
XLA Ops:
  0.7 69.8 %shard_map.82 = f32[1,2,2,256,256]{4,3,2,1,0:T(8,128)S(1)} custom-call(f32[2,256]{1,0:T(2,128)} %onsite.1, f32[2,256,256]{2,1,0:T(8,128)} %hop_in.1, f32[2,256,256]{2,1,0:T(8,128)} %coup_in.1, f32[1]{0:T(128)S(6)} %copy.11.broad, f32[1,2,2,256,256]{4,3,2,1,0:T(8,128)} %born_in.1, s32[4]{0:T(128)} %shift.1, f32[4,256,256]{2,1,0:T(8,128)} %ploc_in.1, ...), custom_call_target="tpu_custom_call" | custom-call | flops 12079595520 | bytes 6291456 | tf_op jit(solution)/shard_map/pallas_call | solution.py:517
  70.5 1.0 %copy.10 = f32[1,2,2,256,256]{4,3,2,1,0:T(8,128)} copy(f32[1,2,2,256,256]{4,3,2,1,0:T(8,128)S(1)} %shard_map.82) | data formatting | bytes 2097152
